TPU v7x, 512 devices: a whole 4x4x16 slice. The times are simulated.
512 devices in a mesh: tm: 32 (over z, core), pairs: 16 (over y, x).
Axes of the slice: x: 4, y: 4, z: 16, core: 2. Of those that a mesh axis runs over, the one named last changes fastest.
Arguments:
- raw_spectra: bfloat16 [32, 2048, 8192], P('tm', 'pairs'), may hold values from -14 to 14, as said below
- tile_chan: int32 [28, 24], replicated, may hold values from 0 to 2047, as said below
- tile_home: int32 [28], replicated, may hold values from 0 to 15, as said below
- block_home: int32 [16], replicated, may hold values from 0 to 15, each once
Outputs:
- stacks: float32 [16, 512, 512], P('pairs', 'tm')
Inputs may be any that keep to these rules, and one draw needn't show every extreme that they name: `raw_spectra`: values lie within the range, with band levels that differ from band to band. `tile_chan`: pairs of a tile are each of its 16 row channels with each of its 8 column channels. All tiles of one device name the same row channels and channels of the same 8 consecutive channel blocks. For each device along pairs, the channels named by its tiles, counted once for each tile that names them, number at most 12 among those held by any one device, and the distinct ones at most 6; both bounds are reached in every draw. `tile_home`: at most 4 tiles belong to one device, and some device owns exactly 4.
All inputs are finite; a program needn't handle non-finite values.
Results may differ from a plain program's by a relative error of at most 0.0059.
Values may be sent and summed in bfloat16 or wider, within the bound.
No kernel may reach another device: no remote copies, remote signals or barrier semaphores. Data moves between devices by JAX's collectives and lax.ppermute only.
A program may use at most 128 MiB of HBM per device.

v0:
```python
import math

import jax
import jax.numpy as jnp
from jax import lax
from jax.sharding import PartitionSpec as P

LAGS = 512
BAND = 128
TILE_ROWS = 16
TILE_COLS = 8
TILE_SLOTS = 4


def whiten(raw):
    values = raw.astype(jnp.float32)
    half_bins = values.shape[-1] // 2
    banded = values.reshape(values.shape[:-1] + (2, half_bins // BAND, BAND))
    band_power = jnp.sum(banded * banded, axis=(-3, -1), keepdims=True) / BAND
    return (banded * lax.rsqrt(band_power + 1e-06)).reshape(values.shape).astype(jnp.bfloat16)


def make_lags(half_bins, segments):
    bin_index = jnp.arange(half_bins, dtype=jnp.int32)
    lag_index = jnp.arange(LAGS, dtype=jnp.int32) - LAGS // 2
    phase_step = jnp.mod(bin_index[:, None] * lag_index[None, :], 2 * half_bins)
    radians = phase_step.astype(jnp.float32) * (math.pi / half_bins)
    norm_scale = 1.0 / math.sqrt(half_bins * segments)
    return (jnp.concatenate([jnp.cos(radians), -jnp.sin(radians)], axis=0) * norm_scale).astype(
        jnp.bfloat16
    )


def slot_table(tile_home, devices, slots):
    onehot = (tile_home[:, None] == jnp.arange(devices, dtype=jnp.int32)[None, :]).astype(jnp.int32)
    tile_rank = jnp.sum((jnp.cumsum(onehot, axis=0) - 1) * onehot, axis=1)
    slot_match = (
        tile_home[None, None, :] == jnp.arange(devices, dtype=jnp.int32)[:, None, None]
    ) & (tile_rank[None, None, :] == jnp.arange(slots, dtype=jnp.int32)[None, :, None])
    return slot_match.astype(jnp.int32)


def cross_terms(rows_a, rows_b):
    a_vals = rows_a.astype(jnp.float32)
    b_vals = rows_b.astype(jnp.float32)
    half_bins = a_vals.shape[-1] // 2
    a_real = a_vals[..., :, None, :half_bins]
    a_imag = a_vals[..., :, None, half_bins:]
    b_real = b_vals[..., None, :, :half_bins]
    b_imag = b_vals[..., None, :, half_bins:]
    return jnp.concatenate(
        [a_real * b_real + a_imag * b_imag, a_real * b_imag - a_imag * b_real], axis=-1
    )


def positions(holder, is_sent, devices):
    onehot = (
        (holder[:, :, None] == jnp.arange(devices, dtype=jnp.int32)[None, None, :])
        & is_sent[:, :, None]
    ).astype(jnp.int32)
    return jnp.sum((jnp.cumsum(onehot, axis=1) - 1) * onehot, axis=2)


def outgoing_rows(local_rows, holder, offset, is_sent, position, my_index, capacity):
    mine_sent = (holder == my_index) & is_sent
    pick_slot = (
        position[:, :, None] == jnp.arange(capacity, dtype=jnp.int32)[None, None, :]
    ) & mine_sent[:, :, None]
    source = jnp.sum(pick_slot * (offset[:, :, None] + 1), axis=1) - 1
    chosen_rows = jnp.take(local_rows, jnp.maximum(source, 0), axis=1)
    return jnp.where((source >= 0)[None, :, :, None], chosen_rows, jnp.zeros((), jnp.bfloat16))


def shards(raw_spectra, tile_chan, tile_home, block_home):
    npairs = lax.axis_size("pairs")
    my_index = lax.axis_index("pairs")
    seg_dev, ch_dev, row_width = raw_spectra.shape
    block_span = npairs // 2
    per_tile = TILE_ROWS + TILE_COLS
    references = TILE_SLOTS * per_tile
    slot_match = slot_table(tile_home, npairs, TILE_SLOTS)
    channel = jnp.einsum("dsk,kr->dsr", slot_match, tile_chan).reshape(npairs, references)
    is_live = jnp.broadcast_to(
        (jnp.sum(slot_match, axis=2) > 0)[:, :, None], (npairs, TILE_SLOTS, per_tile)
    ).reshape(npairs, references)
    channel_block = channel // ch_dev
    holder = jnp.sum(
        (channel_block[:, :, None] == jnp.arange(npairs, dtype=jnp.int32)[None, None, :])
        * block_home[None, None, :],
        axis=2,
    )
    offset = channel % ch_dev
    local_rows = whiten(raw_spectra)
    capacity = references // block_span
    position = positions(holder, is_live, npairs)
    outgoing = outgoing_rows(local_rows, holder, offset, is_live, position, my_index, capacity)
    incoming = lax.all_to_all(outgoing, "pairs", split_axis=1, concat_axis=1, tiled=True)
    received = incoming.reshape(seg_dev, npairs * capacity, row_width)
    wanted = holder[my_index] * capacity + position[my_index]
    picked = jnp.take(received, wanted, axis=1)
    picked = jnp.where(is_live[my_index][None, :, None], picked, jnp.zeros((), jnp.bfloat16))
    picked = picked.reshape(seg_dev, TILE_SLOTS, per_tile, row_width)

    def tile_cross(tile_refs):
        terms = cross_terms(tile_refs[:, :TILE_ROWS], tile_refs[:, TILE_ROWS:])
        return jnp.sum(terms, axis=0).reshape(TILE_ROWS * TILE_COLS, row_width).astype(jnp.bfloat16)

    cross_stack = lax.map(tile_cross, jnp.moveaxis(picked, 1, 0)).reshape(
        TILE_SLOTS * TILE_ROWS * TILE_COLS, row_width
    )
    lag_table = make_lags(row_width // 2, seg_dev * lax.axis_size("tm"))
    rows_kept = cross_stack.shape[0] // lax.axis_size("tm")
    stacked = lax.psum_scatter(
        jnp.dot(cross_stack, lag_table, preferred_element_type=jnp.float32),
        "tm",
        scatter_dimension=0,
        tiled=True,
    )
    return stacked.reshape(1, rows_kept, LAGS)


def solution(mesh):
    return jax.shard_map(
        shards,
        mesh=mesh,
        in_specs=(P("tm", "pairs", None), P(), P(), P()),
        out_specs=P("pairs", "tm", None),
        check_vma=False,
    )
```

profile of v0, /device:TPU:2, one launch (start us, length us, event | category | flops | bytes accessed | tf_op | source)
XLA Modules:
  0.0 265.0 jit_solution(10682212035502854762)
XLA Ops:
  6.5 0.0 copy-start
  6.5 0.7 iota_compare_fusion.4
  7.2 0.7 fusion.26
  7.9 0.1 reduce_window_sum.22
  8.0 0.8 select_reduce_fusion.3
  8.8 0.2 fusion.25
  9.0 0.0 copy-done
  9.0 0.2 fusion.23
  9.2 0.1 reshape.392
  9.3 0.1 copy.35
  9.4 2.6 select_reduce_fusion.1
  12.0 0.1 copy.37
  12.1 2.5 select_reduce_fusion
  14.6 0.1 copy.36
  14.7 0.3 select_reduce_fusion.2
  15.0 0.1 copy.40
  15.1 0.1 reshape.400
  15.2 0.1 copy.38
  15.3 0.1 copy.39
  15.4 2.0 fusion.12
  17.4 2.7 %copy.43 = f32[16,8,64,128]{3,2,1,0:T(8,128)} copy(f32[16,8,64,128]{3,1,2,0:T(8,128)S(1)} %fusion.12) | data formatting | bytes 8388608
  20.1 2.8 %reduce_sum.63 = f32[128,32]{1,0:T(8,128)S(1)} reduce(f32[128,2,32,128]{3,2,1,0:T(8,128)} %bitcast.50, f32[]{:T(128)} %constant.117.clone.1), dimensions={1,3}, to_apply=%region_7.8 | reduce | flops 1044480 | bytes 4210692 | tf_op jit(solution)/shard_map/reduce_sum | solution.py:19
  22.9 2.5 mul.206
  25.5 5.0 %mul.207 = f32[1,128,8192]{2,1,0:T(8,128)} reshape(f32[128,2,32,128]{3,2,1,0:T(8,128)} %mul.206) | data formatting | bytes 8388608 | tf_op jit(solution)/shard_map/mul | solution.py:20
  30.4 3.3 %fusion.15 = bf16[128,8192]{1,0:T(8,128)(2,1)S(1)} fusion(f32[1,128,8192]{2,1,0:T(8,128)} %mul.207, bf16[1,128,8192]{2,1,0:T(8,128)(2,1)} %param.6), kind=kLoop, calls=%fused_computation.34 | loop fusion | flops 3145728 | bytes 8388608 | tf_op jit(solution)/shard_map/convert_element_type | solution.py:20
  33.7 4.2 %gather_fusion = bf16[192,8192]{1,0:T(8,128)(2,1)} fusion(bf16[128,8192]{1,0:T(8,128)(2,1)S(1)} %fusion.15, s32[1024]{0:T(1024)S(1)} %pad_clamp_fusion.1), kind=kCustom, calls=%fused_computation | custom fusion | bytes 6292224 | tf_op jit(solution)/shard_map/jit(_take)/gather | solution.py:70
  37.9 4.7 %reshape.397 = bf16[1,16,12,8192]{3,2,1,0:T(8,128)(2,1)} reshape(bf16[192,8192]{1,0:T(8,128)(2,1)} %gather_fusion) | data formatting | bytes 6291456 | tf_op jit(solution)/shard_map/jit(_take)/gather | solution.py:70
  42.7 4.7 %select_bitcast_fusion = bf16[1,16,12,8192]{3,2,0,1:T(8,128)(2,1)} fusion(bf16[1,16,12,8192]{3,2,1,0:T(8,128)(2,1)} %reshape.397, pred[16,12]{1,0:T(8,128)(4,1)S(1)} %copy.39, pred[16,12]{1,0:T(8,128)(4,1)S(1)} %copy.38), kind=kLoop, calls=%fused_computation.33 | loop fusion | flops 3145728 | bytes 6291840 | tf_op jit(solution)/shard_map/jit(_where)/select_n | solution.py:71
  47.3 10.2 %all-to-all-start = ((bf16[1,16,12,8192]{3,2,0,1:T(8,128)(2,1)}), bf16[1,16,12,8192]{3,2,0,1:T(8,128)(2,1)}, u32[]{:S(2)}, u32[]{:S(2)}) async-start(bf16[1,16,12,8192]{3,2,0,1:T(8,128)(2,1)} %select_bitcast_fusion), calls=%async_computation | async-start | bytes 8388608 | tf_op jit(solution)/shard_map/all_to_all | solution.py:97
  57.5 0.2 reduce-scatter.2.cloned.1.call-start
  57.7 0.2 dynamic-slice_reduce_fusion
  57.9 0.1 broadcast_in_dim.53
  58.0 0.2 add_reduce_fusion
  58.2 0.1 add.135
  58.3 34.6 %fusion.14 = (f32[4096,512]{1,0:T(8,128)}, f32[4096,512]{1,0:T(8,128)}) fusion(s32[512]{0:T(512)S(1)} %iota_add_fusion), kind=kLoop, calls=%fused_computation.32 | loop fusion | flops 31457280 | bytes 16779264 | tf_op jit(solution)/shard_map/cos | solution.py:29
  92.9 15.9 %all-to-all-done = bf16[1,16,12,8192]{3,2,0,1:T(8,128)(2,1)} async-done(((bf16[1,16,12,8192]{3,2,0,1:T(8,128)(2,1)}), bf16[1,16,12,8192]{3,2,0,1:T(8,128)(2,1)}, u32[]{:S(2)}, u32[]{:S(2)}) %all-to-all-start) | async-done | bytes 3145760 | tf_op jit(solution)/shard_map/all_to_all | solution.py:97
  108.8 3.2 %reshape.406 = bf16[192,8192]{1,0:T(8,128)(2,1)S(1)} reshape(bf16[1,16,12,8192]{3,2,0,1:T(8,128)(2,1)} %all-to-all-done) | data formatting | bytes 6291456 | tf_op jit(solution)/shard_map/reshape | solution.py:98
  112.1 2.8 %gather_fusion.1 = bf16[96,8192]{1,0:T(8,128)(2,1)} fusion(bf16[192,8192]{1,0:T(8,128)(2,1)S(1)} %reshape.406, s32[1024]{0:T(1024)S(1)} %pad_clamp_fusion), kind=kCustom, calls=%fused_computation.1 | custom fusion | bytes 3146112 | tf_op jit(solution)/shard_map/jit(_take)/gather | solution.py:100
  114.8 1.6 select_select_fusion
  116.5 8.8 %while.10 = (s32[]{:T(128)}, bf16[4,128,8192]{2,1,0:T(8,128)(2,1)}, bf16[4,1,24,8192]{3,2,1,0:T(8,128)(2,1)S(1)}, s32[]{:T(128)}) while((s32[]{:T(128)}, bf16[4,128,8192]{2,1,0:T(8,128)(2,1)}, bf16[4,1,24,8192]{3,2,1,0:T(8,128)(2,1)S(1)}, s32[]{:T(128)}) %tuple.30), condition=%wide.region_9.10_spmd, body=%wide.region_8.9_spmd.sunk | while | flops 8585218 | bytes 10616901 | solution.py:108
  116.7 0.5 fusion.38
  117.2 1.5 maximum_dynamic-update-slice_fusion.2
  118.9 0.5 fusion.38
  119.4 1.5 maximum_dynamic-update-slice_fusion.2
  121.1 0.5 fusion.38
  121.5 1.5 maximum_dynamic-update-slice_fusion.2
  123.2 0.5 fusion.38
  123.7 1.5 maximum_dynamic-update-slice_fusion.2
  125.3 0.0 copy-start.1
  125.3 13.7 %fusion.6 = f32[512,512]{1,0:T(8,128)} fusion(bf16[512,8192]{1,0:T(8,128)(2,1)} %bitcast.54, f32[4096,512]{1,0:T(8,128)} %get-tuple-element.40, f32[4096,512]{1,0:T(8,128)} %get-tuple-element.39), kind=kOutput, calls=%fused_computation.22 | convolution fusion | flops 4307550208 | bytes 26214400 | tf_op jit(solution)/shard_map/dot_general | solution.py:114
  139.0 0.0 reduce-scatter.2.cloned.1.call-update
  139.0 119.1 %reduce-scatter.2.cloned.1.call-done = f32[16,512]{1,0:T(8,128)} async-done(((f32[512,512]{1,0:T(8,128)}), f32[16,512]{1,0:T(8,128)}) %reduce-scatter.2.cloned.1.call-update) | async-done | bytes 32784 | tf_op jit(solution)/shard_map/reduce_scatter | solution.py:113
  258.1 0.0 copy-done.1
  (35 shorter events, 0.7 us)
Async XLA Ops:
  6.5 2.5 copy-start
  47.3 61.5 %all-to-all-start = ((bf16[1,16,12,8192]{3,2,0,1:T(8,128)(2,1)}), bf16[1,16,12,8192]{3,2,0,1:T(8,128)(2,1)}, u32[]{:S(2)}, u32[]{:S(2)}) async-start(bf16[1,16,12,8192]{3,2,0,1:T(8,128)(2,1)} %select_bitcast_fusion), calls=%async_computation | async-start | bytes 8388608 | tf_op jit(solution)/shard_map/all_to_all | solution.py:97
  57.5 200.6 %reduce-scatter.2.cloned.1.call-start = ((), (), s32[]{:S(2)}) async-start(), calls=%async_computation.2 | async-start | bytes 1081344 | tf_op jit(solution)/shard_map/reduce_scatter | solution.py:113
  125.3 132.9 %copy-start.1 = (s32[28,24]{0,1:T(8,128)S(1)}, s32[28,24]{0,1:T(8,128)}, u32[]{:S(2)}) copy-start(s32[28,24]{0,1:T(8,128)} %param.7) | copy-start | bytes 8068
Sparse Core Ops, SparseCore 0:
  139.1 118.9 reduce-scatter.1
where the time goes:
time: 266 us; the launch traced here: 265 us
  waiting for transfers between devices  135 us (51%)
  other arithmetic  65.5 us (25%)
  local copies, waits for them, and re-layouts  26.5 us (10%)
  matrix products  13.9 us (5%)
  between operations  13.6 us (5%)
  starting transfers between devices  10.4 us (4%)
    reduce_scatter x1, waiting for transfers between devices, shards(): lax.psum_scatter(jnp.dot(cross_stack, lag_table, preferred_element_type=j...  119 us
    cos x1, other arithmetic, make_lags(): jnp.cos(radians)  34.6 us
    all_to_all x1, waiting for transfers between devices, shards(): lax.all_to_all(outgoing, 'pairs', split_axis=1, concat_axis=1, tiled=True)  15.9 us
    dot_general x1, matrix products, shards(): jnp.dot(cross_stack, lag_table, preferred_element_type=jnp.float32)  13.7 us
    all_to_all x1, starting transfers between devices, shards(): lax.all_to_all(outgoing, 'pairs', split_axis=1, concat_axis=1, tiled=True)  10.2 us
    gather x2, local copies, waits for them, and re-layouts, outgoing_rows(): chosen_rows = jnp.take(local_rows, jnp.maximum(source, 0), axis=1)  8.95 us
    mul x2, local copies, waits for them, and re-layouts, whiten(): banded * lax.rsqrt(band_power + 1e-06)  7.5 us
    dynamic_update_slice x4, other arithmetic, shards(): lax.map(tile_cross, jnp.moveaxis(picked, 1, 0))  6.08 us
  transfers between devices with their start and end apart: 2, of which 2 were waited for; matrix products, arithmetic and copies ran while one was open for 13% of the time, Pallas kernels for 0%

commit v1 on v0

v1 whole, which is shorter than its diff:
```python
import functools
import math

import jax
import jax.numpy as jnp
import ml_dtypes
import numpy as np
from jax import lax
from jax.experimental import pallas as pl
from jax.experimental.pallas import tpu as pltpu
from jax.sharding import Mesh
from jax.sharding import PartitionSpec as P

LAGS = 512
BAND = 128
TILE_ROWS = 16
TILE_COLS = 8
TILE_SLOTS = 4
PER_TILE = TILE_ROWS + TILE_COLS
REFS = TILE_SLOTS * PER_TILE
PAIRS = TILE_ROWS * TILE_COLS
CAP = 6
GROUPS = 4
CHUNK = CAP * GROUPS
STEPS = 4
HALF = LAGS // 2
F32 = jnp.float32
BF16 = jnp.bfloat16


def iota(shape, dim):
    return lax.broadcasted_iota(jnp.int32, shape, dim)


def before(size):
    return (iota((size, size), 0) < iota((size, size), 1)).astype(BF16)


def send_kernel(home_ref, block_ref, chan_ref, re_ref, im_ref, out_ref, pick_ref):
    owners = block_ref.shape[0]
    channels = re_ref.shape[1]
    sub = re_ref.shape[2] // GROUPS

    @pl.when(pl.program_id(0) == 0)
    def _():
        me = lax.axis_index("pairs")
        block = jnp.int32(0)
        for b in range(owners):
            block = jnp.where(block_ref[b] == me, b, block)
        chan = chan_ref[...]
        offset = iota((PER_TILE, channels), 1) + block * channels
        owner = iota((owners, channels), 0)
        named = jnp.zeros((owners, channels), F32)
        for t in range(home_ref.shape[0]):
            hit = jnp.max((chan[:, t : t + 1] == offset).astype(F32), axis=0, keepdims=True)
            named = jnp.maximum(named, jnp.where(owner == home_ref[t], hit, 0.0))
        rank = jnp.dot(named.astype(BF16), before(channels), preferred_element_type=F32)
        key = jnp.where(named > 0.0, rank, -1.0)
        row = iota((CHUNK, channels), 0)
        place = (row % CAP).astype(F32)
        group = row // CAP
        parts = []
        for p in range(owners):
            match = jnp.broadcast_to(key[p : p + 1, :], (CHUNK, channels)) == place
            parts.append(
                jnp.concatenate(
                    [jnp.where(match & (group == g), 1.0, 0.0) for g in range(GROUPS)], axis=1
                )
            )
        pick_ref[...] = jnp.concatenate(parts, axis=0).astype(BF16)

    stacked = jnp.concatenate(
        [
            jnp.concatenate(
                [re_ref[0, :, g * sub : (g + 1) * sub], im_ref[0, :, g * sub : (g + 1) * sub]],
                axis=1,
            )
            for g in range(GROUPS)
        ],
        axis=0,
    )
    out_ref[...] = jnp.dot(pick_ref[...], stacked, preferred_element_type=F32).astype(BF16)


def send_rows(raw, chan, tile_home, block_home):
    _, channels, width = raw.shape
    owners = block_home.shape[0]
    wide = width // (2 * STEPS)
    return pl.pallas_call(
        send_kernel,
        grid=(STEPS,),
        in_specs=[
            pl.BlockSpec(memory_space=pltpu.SMEM),
            pl.BlockSpec(memory_space=pltpu.SMEM),
            pl.BlockSpec(chan.shape, lambda i: (0, 0)),
            pl.BlockSpec((1, channels, wide), lambda i: (0, 0, i)),
            pl.BlockSpec((1, channels, wide), lambda i: (0, 0, i + STEPS)),
        ],
        out_specs=pl.BlockSpec((owners * CHUNK, 2 * wide // GROUPS), lambda i: (0, i)),
        out_shape=jax.ShapeDtypeStruct((owners * CHUNK, width // GROUPS), BF16),
        scratch_shapes=[pltpu.VMEM((owners * CHUNK, GROUPS * channels), BF16)],
        compiler_params=pltpu.CompilerParams(vmem_limit_bytes=32 * 1024 * 1024),
        name="send_rows",
    )(tile_home, block_home, chan, raw, raw)


def table_kernel(scale, home_ref, block_ref, chan_ref, lag_ref, place_ref, cos_ref, sin_ref):
    step = pl.program_id(0)
    rows = lag_ref.shape[0]
    low = cos_ref.shape[0]
    high = rows // low
    turn = 2 * rows * STEPS

    def angles(count, first, stride):
        freq = (iota((count, HALF), 0) + first) * stride
        lag = iota((count, HALF), 1) + 1
        return ((freq * lag) & (turn - 1)).astype(F32) * (2.0 * math.pi / turn)

    @pl.when(step == 0)
    def _():
        angle = angles(low, 0, 1)
        cos_ref[...] = jnp.cos(angle)
        sin_ref[...] = jnp.sin(angle)
        me = lax.axis_index("pairs")
        chan = chan_ref[...]
        lane = iota(chan.shape, 1)
        columns = []
        for s in range(TILE_SLOTS):
            tile = jnp.int32(-1)
            seen = jnp.int32(0)
            for t in range(home_ref.shape[0]):
                mine = home_ref[t] == me
                tile = jnp.where(mine & (seen == s), t, tile)
                seen = seen + mine.astype(jnp.int32)
            column = jnp.sum(jnp.where(lane == tile, chan + 1, 0), axis=1, keepdims=True)
            columns.append(column - 1)
        named = jnp.broadcast_to(jnp.concatenate(columns, axis=0), (REFS, BAND))
        cell = iota((REFS, BAND), 1)
        in_block = (named >= 0) & ((named // BAND) == cell)
        at_offset = (named >= 0) & ((named % BAND) == cell)
        block_hot = in_block.astype(F32).astype(BF16)
        offset_hot = at_offset.astype(F32)
        count = lax.dot_general(
            block_hot, offset_hot.astype(BF16), (((0,), (0,)), ((), ())), preferred_element_type=F32
        )
        rank = jnp.dot(
            (count > 0.0).astype(F32).astype(BF16), before(BAND), preferred_element_type=F32
        )
        own_rank = jnp.dot(block_hot, rank.astype(BF16), preferred_element_type=F32)
        position = jnp.sum(own_rank * offset_hot, axis=1, keepdims=True).astype(jnp.int32)
        holder = jnp.zeros((REFS, BAND), jnp.int32)
        for b in range(block_ref.shape[0]):
            holder = jnp.where((named // BAND) == b, block_ref[b], holder)
        place_ref[...] = jnp.where(named >= 0, holder * CHUNK + position, -CHUNK)

    coarse = angles(high, step * high, low)
    cos_high = jnp.cos(coarse) * scale
    sin_high = jnp.sin(coarse) * scale
    cos_low = cos_ref[...]
    sin_low = sin_ref[...]
    for q in range(high):
        ch = cos_high[q : q + 1, :]
        sh = sin_high[q : q + 1, :]
        rows_q = slice(q * low, (q + 1) * low)
        lag_ref[rows_q, :HALF] = (ch * cos_low - sh * sin_low).astype(BF16)
        lag_ref[rows_q, HALF:] = (sh * cos_low + ch * sin_low).astype(BF16)


def tables(bins, segments, chan, tile_home, block_home):
    rows = bins // STEPS
    low = 64
    return pl.pallas_call(
        functools.partial(table_kernel, 1.0 / math.sqrt(bins * segments)),
        grid=(STEPS,),
        in_specs=[
            pl.BlockSpec(memory_space=pltpu.SMEM),
            pl.BlockSpec(memory_space=pltpu.SMEM),
            pl.BlockSpec(chan.shape, lambda i: (0, 0)),
        ],
        out_specs=[
            pl.BlockSpec((rows, LAGS), lambda i: (i, 0)),
            pl.BlockSpec((REFS, BAND), lambda i: (0, 0)),
        ],
        out_shape=[
            jax.ShapeDtypeStruct((bins, LAGS), BF16),
            jax.ShapeDtypeStruct((REFS, BAND), jnp.int32),
        ],
        scratch_shapes=[pltpu.VMEM((low, HALF), F32), pltpu.VMEM((low, HALF), F32)],
        compiler_params=pltpu.CompilerParams(vmem_limit_bytes=32 * 1024 * 1024),
        cost_estimate=pl.CostEstimate(flops=20_000_000, bytes_accessed=8_000_000, transcendentals=0),
        name="tables",
    )(tile_home, block_home, chan)


def stack_kernel(
    zero_scale, place_ref, got_ref, lag_ref, keep_ref, send_ref,
    cross_re, cross_im, even_ref, odd_ref, zero_ref, both_ref,
):
    step = pl.program_id(0)
    sub = got_ref.shape[1] // 2
    received = got_ref.shape[0]

    @pl.when(step == 0)
    def _():
        even_ref[...] = jnp.zeros_like(even_ref)
        odd_ref[...] = jnp.zeros_like(odd_ref)
        zero_ref[...] = jnp.zeros_like(zero_ref)

    white_re, white_im = [], []
    for band in range(sub // BAND):
        re = got_ref[:, band * BAND : (band + 1) * BAND].astype(F32)
        im = got_ref[:, sub + band * BAND : sub + (band + 1) * BAND].astype(F32)
        power = jnp.sum(re * re + im * im, axis=1, keepdims=True) * (1.0 / BAND)
        scale = lax.rsqrt(power + 1e-06)
        white_re.append((re * scale).astype(BF16))
        white_im.append((im * scale).astype(BF16))
    white = jnp.concatenate(white_re + white_im, axis=1)

    place = place_ref[...]
    column = iota((REFS, BAND), 1)
    for g in range(GROUPS):
        chosen = jnp.concatenate(
            [
                jnp.where(column + k * BAND == place + g * CAP, 1.0, 0.0)
                for k in range(received // BAND)
            ],
            axis=1,
        ).astype(BF16)
        rows = jnp.dot(chosen, white, preferred_element_type=F32)
        for s in range(TILE_SLOTS):
            top = s * PER_TILE
            b_re = rows[top + TILE_ROWS : top + PER_TILE, :sub]
            b_im = rows[top + TILE_ROWS : top + PER_TILE, sub:]
            re_parts, im_parts = [], []
            for i in range(TILE_ROWS):
                a_re = rows[top + i : top + i + 1, :sub]
                a_im = rows[top + i : top + i + 1, sub:]
                re_parts.append(a_re * b_re + a_im * b_im)
                im_parts.append(a_re * b_im - a_im * b_re)
            re_all = jnp.concatenate(re_parts, axis=0)
            im_all = jnp.concatenate(im_parts, axis=0)
            span = slice(s * PAIRS, (s + 1) * PAIRS)
            folded = re_all[:, :BAND]
            for band in range(1, sub // BAND):
                folded = folded + re_all[:, band * BAND : (band + 1) * BAND]
            zero_ref[span, :] += folded
            cross_re[span, g * sub : (g + 1) * sub] = re_all.astype(BF16)
            cross_im[span, g * sub : (g + 1) * sub] = im_all.astype(BF16)
    even_ref[...] += jnp.dot(cross_re[...], lag_ref[:, :HALF], preferred_element_type=F32)
    odd_ref[...] += jnp.dot(cross_im[...], lag_ref[:, HALF:], preferred_element_type=F32)

    @pl.when(step == pl.num_programs(0) - 1)
    def _():
        core = lax.axis_index("core")
        even = even_ref[...]
        odd = odd_ref[...]
        at_zero = jnp.sum(zero_ref[...], axis=1, keepdims=True) * zero_scale
        behind = even + odd
        ahead = pltpu.roll(even - odd, 1, 1)
        ahead = jnp.where(iota(ahead.shape, 1) == 0, at_zero, ahead)
        kept = both_ref.shape[2]
        for z in range(both_ref.shape[1]):
            for c in range(2):
                first = (2 * z + c) * kept
                side = jnp.bitwise_xor(core, c)
                both_ref[side, z, :, :HALF] = behind[first : first + kept]
                both_ref[side, z, :, HALF:] = ahead[first : first + kept]
        keep_ref[...] = both_ref[0]
        send_ref[...] = both_ref[1].astype(BF16)


def stack(place, got, lag, depth, segments):
    received, width = got.shape
    bins = lag.shape[0]
    pairs = TILE_SLOTS * PAIRS
    kept = pairs // (2 * depth)
    zero_scale = float(np.float32(1.0 / math.sqrt(bins * segments)).astype(ml_dtypes.bfloat16))
    shape = (depth, kept, LAGS)
    return pl.pallas_call(
        functools.partial(stack_kernel, zero_scale),
        grid=(STEPS,),
        in_specs=[
            pl.BlockSpec((REFS, BAND), lambda i: (0, 0)),
            pl.BlockSpec((received, width // STEPS), lambda i: (0, i)),
            pl.BlockSpec((bins // STEPS, LAGS), lambda i: (i, 0)),
        ],
        out_specs=[
            pl.BlockSpec(shape, lambda i: (0, 0, 0)),
            pl.BlockSpec(shape, lambda i: (0, 0, 0)),
        ],
        out_shape=[jax.ShapeDtypeStruct(shape, F32), jax.ShapeDtypeStruct(shape, BF16)],
        scratch_shapes=[
            pltpu.VMEM((pairs, bins // STEPS), BF16),
            pltpu.VMEM((pairs, bins // STEPS), BF16),
            pltpu.VMEM((pairs, HALF), F32),
            pltpu.VMEM((pairs, HALF), F32),
            pltpu.VMEM((pairs, BAND), F32),
            pltpu.VMEM((2,) + shape, F32),
        ],
        compiler_params=pltpu.CompilerParams(vmem_limit_bytes=48 * 1024 * 1024),
        name="stack",
    )(place, got, lag)


def finish_kernel(parts_ref, out_ref):
    total = parts_ref[0].astype(F32)
    for z in range(1, parts_ref.shape[0]):
        total = total + parts_ref[z].astype(F32)
    mirror = (iota((HALF, HALF), 0) + iota((HALF, HALF), 1) == HALF - 1).astype(F32)
    out_ref[0, :, :HALF] = jnp.dot(
        total[:, :HALF], mirror, precision=lax.Precision.HIGHEST, preferred_element_type=F32
    )
    out_ref[0, :, HALF:] = total[:, HALF:]


def finish(parts):
    _, kept, lags = parts.shape
    return pl.pallas_call(
        finish_kernel,
        out_shape=jax.ShapeDtypeStruct((1, kept, lags), F32),
        name="finish",
    )(parts)


def shards(raw_spectra, tile_chan, tile_home, block_home):
    depth = lax.axis_size("z")
    segments = 2 * depth
    bins = raw_spectra.shape[2] // 2
    chan = tile_chan.T
    outgoing = send_rows(raw_spectra, chan, tile_home, block_home)
    owners = block_home.shape[0]
    incoming = lax.all_to_all(
        outgoing.reshape(owners, CHUNK, -1), "pairs", split_axis=0, concat_axis=0, tiled=True
    )
    lag, place = tables(bins, segments, chan, tile_home, block_home)
    keep, send = stack(place, incoming.reshape(outgoing.shape), lag, depth, segments)
    swapped = lax.ppermute(send, "core", [(0, 1), (1, 0)])
    both = (keep + swapped.astype(F32)).astype(BF16)
    parts = lax.all_to_all(both, "z", split_axis=0, concat_axis=0, tiled=True)
    return finish(parts)


def solution(mesh):
    devices = mesh.devices
    split = Mesh(
        devices.reshape(devices.shape[0] // 2, 2, devices.shape[1]), ("z", "core", "pairs")
    )
    return jax.shard_map(
        shards,
        mesh=split,
        in_specs=(P(("z", "core"), "pairs", None), P(), P(), P()),
        out_specs=P("pairs", ("z", "core"), None),
        check_vma=False,
    )
```

time: 266 us -> 84.9 us (0.32)
  the two profiles are of different devices: /device:TPU:2 before, /device:TPU:32 now
where the time goes in v1:
time: 84.9 us; the launch traced here: 84.4 us
  blocking collectives  33.5 us (39%)
  waiting for transfers between devices  20.9 us (25%)
  Pallas kernels  15.2 us (18%)
  starting transfers between devices  9.1 us (11%)
  local copies, waits for them, and re-layouts  5.56 us (7%)
    all_to_all x1, blocking collectives, shards(): parts = lax.all_to_all(both, 'z', split_axis=0, concat_axis=0, tiled=True)  33.5 us
    all_to_all x1, waiting for transfers between devices, shards(): lax.all_to_all(outgoing.reshape(owners, CHUNK, -1), 'pairs', split_axis=0...  19.4 us
    all_to_all x1, starting transfers between devices, shards(): lax.all_to_all(outgoing.reshape(owners, CHUNK, -1), 'pairs', split_axis=0...  7.18 us
    pallas_call x1, Pallas kernels, stack(): pl.pallas_call(functools.partial(stack_kernel, zero_scale), grid=(STEPS,)...  6.58 us
    unnamed x16, local copies, waits for them, and re-layouts  5.56 us
    pallas_call x1, Pallas kernels, send_rows(): pl.pallas_call(send_kernel, grid=(STEPS,), in_specs=[pl.BlockSpec(memory_...  3.78 us
    pallas_call x1, Pallas kernels, tables(): pl.pallas_call(functools.partial(table_kernel, 1.0 / math.sqrt(bins * seg...  3.07 us
    ppermute x1, starting transfers between devices, shards(): swapped = lax.ppermute(send, 'core', [(0, 1), (1, 0)])  1.92 us
  transfers between devices with their start and end apart: 2, of which 2 were waited for; matrix products, arithmetic and copies ran while one was open for 0% of the time, Pallas kernels for 4%

profile of v1, /device:TPU:32, one launch (start us, length us, event | category | flops | bytes accessed | tf_op | source)
XLA Modules:
  0.0 84.4 jit_solution(13694447276619081578)
XLA Ops:
  0.0 0.0 copy-start
  0.0 1.6 %copy-done = bf16[1,128,8192]{2,1,0:T(8,128)(2,1)S(1)} copy-done((bf16[1,128,8192]{2,1,0:T(8,128)(2,1)S(1)}, bf16[1,128,8192]{2,1,0:T(8,128)(2,1)}, u32[]{:S(2)}) %copy-start) | copy-done | bytes 2097176
  1.6 0.0 copy-start.2
  1.6 0.7 copy-done.2
  2.3 0.0 copy-start.4
  2.3 0.7 copy-done.4
  3.0 0.0 copy-start.6
  3.0 0.7 copy-done.6
  3.6 3.8 %send_rows.1 = bf16[384,2048]{1,0:T(8,128)(2,1)} custom-call(s32[28]{0:T(128)S(1)} %copy-done.4, s32[16]{0:T(128)S(1)} %copy-done.6, s32[24,28]{1,0:T(8,128)S(1)} %bitcast.4, bf16[1,128,8192]{2,1,0:T(8,128)(2,1)S(1)} %copy-done, bf16[1,128,8192]{2,1,0:T(8,128)(2,1)S(1)} %copy-done), custom_call_target="tpu_custom_call" | custom-call | tf_op jit(solution)/shard_map/send_rows/pallas_call | solution.py:89
  7.4 0.0 copy-start.3
  7.4 0.0 copy-start.5
  7.4 0.0 copy-start.7
  7.4 7.2 %all-to-all-start = ((bf16[16,24,2048]{2,1,0:T(8,128)(2,1)}), bf16[16,24,2048]{2,1,0:T(8,128)(2,1)S(1)}, u32[]{:S(2)}, u32[]{:S(2)}) async-start(bf16[16,24,2048]{2,1,0:T(8,128)(2,1)} %bitcast.1), calls=%async_computation | async-start | bytes 3145728 | tf_op jit(solution)/shard_map/all_to_all | solution.py:332
  14.6 0.0 copy-done.3
  14.6 0.0 copy-done.5
  14.6 0.0 copy-done.7
  14.6 3.1 %tables.1 = (bf16[4096,512]{1,0:T(8,128)(2,1)S(1)}, s32[96,128]{1,0:T(8,128)S(1)}) custom-call(s32[28]{0:T(128)S(1)} %copy-done.5, s32[16]{0:T(128)S(1)} %copy-done.7, s32[24,28]{1,0:T(8,128)S(1)} %bitcast.5), custom_call_target="tpu_custom_call" | custom-call | flops 20000000 | bytes 8000000 | tf_op jit(solution)/shard_map/tables/pallas_call | solution.py:172
  17.7 0.0 copy-start.1
  17.7 1.9 %copy-done.1 = bf16[4096,512]{1,0:T(8,128)(2,1)} copy-done((bf16[4096,512]{1,0:T(8,128)(2,1)}, bf16[4096,512]{1,0:T(8,128)(2,1)S(1)}, u32[]{:S(2)}) %copy-start.1) | copy-done | bytes 4194328
  19.6 19.4 %all-to-all-done = bf16[16,24,2048]{2,1,0:T(8,128)(2,1)S(1)} async-done(((bf16[16,24,2048]{2,1,0:T(8,128)(2,1)}), bf16[16,24,2048]{2,1,0:T(8,128)(2,1)S(1)}, u32[]{:S(2)}, u32[]{:S(2)}) %all-to-all-start) | async-done | bytes 1572896 | tf_op jit(solution)/shard_map/all_to_all | solution.py:332
  39.0 6.6 %stack.1 = (f32[16,16,512]{2,1,0:T(8,128)S(1)}, bf16[16,16,512]{2,1,0:T(8,128)(2,1)S(1)}) custom-call(s32[96,128]{1,0:T(8,128)S(1)} %get-tuple-element.9.place_ref, bf16[384,2048]{1,0:T(8,128)(2,1)S(1)} %bitcast.3, bf16[4096,512]{1,0:T(8,128)(2,1)} %copy-done.1), custom_call_target="tpu_custom_call" | custom-call | tf_op jit(solution)/shard_map/stack/pallas_call | solution.py:279
  45.6 1.9 %collective-permute-start = (bf16[16,16,512]{2,1,0:T(8,128)(2,1)S(1)}, bf16[16,16,512]{2,1,0:T(8,128)(2,1)S(1)}, u32[]{:S(2)}, u32[]{:S(2)}) collective-permute-start(bf16[16,16,512]{2,1,0:T(8,128)(2,1)S(1)} %get-tuple-element.12), channel_id=1, source_target_pairs={{0,16},{16,0},{1,17},{17,1},{2,18},{18,2},{3,19},{19,3},{4,20},{20... | collective-permute-start | bytes 786440 | tf_op jit(solution)/shard_map/ppermute | solution.py:337
  47.6 1.5 %collective-permute-done = bf16[16,16,512]{2,1,0:T(8,128)(2,1)S(1)} collective-permute-done((bf16[16,16,512]{2,1,0:T(8,128)(2,1)S(1)}, bf16[16,16,512]{2,1,0:T(8,128)(2,1)S(1)}, u32[]{:S(2)}, u32[]{:S(2)}) %collective-permute-start) | collective-permute-done | bytes 262176 | tf_op jit(solution)/shard_map/ppermute | solution.py:337
  49.1 0.1 add_convert_fusion
  49.2 33.5 %all_to_all.10.parts_ref = bf16[16,16,512]{2,1,0:T(8,128)(2,1)} all-to-all(bf16[16,16,512]{2,1,0:T(8,128)(2,1)S(1)} %add_convert_fusion), channel_id=1, replica_groups=mesh['z'=16,'core'=2,'pairs'=16] {'z'}, dimensions={0} | all-to-all | bytes 524288 | tf_op jit(solution)/shard_map/all_to_all | solution.py:339
  82.6 1.8 %finish.1 = f32[1,16,512]{2,1,0:T(8,128)} custom-call(bf16[16,16,512]{2,1,0:T(8,128)(2,1)} %all_to_all.10.parts_ref), custom_call_target="tpu_custom_call" | custom-call | tf_op jit(solution)/shard_map/finish/pallas_call | solution.py:318
Async XLA Ops:
  0.0 1.6 %copy-start = (bf16[1,128,8192]{2,1,0:T(8,128)(2,1)S(1)}, bf16[1,128,8192]{2,1,0:T(8,128)(2,1)}, u32[]{:S(2)}) copy-start(bf16[1,128,8192]{2,1,0:T(8,128)(2,1)} %im_ref.1) | copy-start | bytes 6291460
  1.6 0.7 copy-start.2
  2.3 0.7 copy-start.4
  3.0 0.7 copy-start.6
  7.4 7.2 %copy-start.3 = (s32[28,24]{0,1:T(8,128)S(1)}, s32[28,24]{0,1:T(8,128)}, u32[]{:S(2)}) copy-start(s32[28,24]{0,1:T(8,128)} %param.5) | copy-start | bytes 8068
  7.4 7.2 %copy-start.5 = (s32[28]{0:T(128)S(1)}, s32[28]{0:T(128)}, u32[]{:S(2)}) copy-start(s32[28]{0:T(128)} %home_ref.3) | copy-start | bytes 340
  7.4 7.2 %copy-start.7 = (s32[16]{0:T(128)S(1)}, s32[16]{0:T(128)}, u32[]{:S(2)}) copy-start(s32[16]{0:T(128)} %block_ref.3) | copy-start | bytes 196
  7.4 31.7 %all-to-all-start = ((bf16[16,24,2048]{2,1,0:T(8,128)(2,1)}), bf16[16,24,2048]{2,1,0:T(8,128)(2,1)S(1)}, u32[]{:S(2)}, u32[]{:S(2)}) async-start(bf16[16,24,2048]{2,1,0:T(8,128)(2,1)} %bitcast.1), calls=%async_computation | async-start | bytes 3145728 | tf_op jit(solution)/shard_map/all_to_all | solution.py:332
  17.7 2.0 %copy-start.1 = (bf16[4096,512]{1,0:T(8,128)(2,1)}, bf16[4096,512]{1,0:T(8,128)(2,1)S(1)}, u32[]{:S(2)}) copy-start(bf16[4096,512]{1,0:T(8,128)(2,1)S(1)} %get-tuple-element.10.lag_ref) | copy-start | bytes 12582916
  45.6 3.4 %collective-permute-start = (bf16[16,16,512]{2,1,0:T(8,128)(2,1)S(1)}, bf16[16,16,512]{2,1,0:T(8,128)(2,1)S(1)}, u32[]{:S(2)}, u32[]{:S(2)}) collective-permute-start(bf16[16,16,512]{2,1,0:T(8,128)(2,1)S(1)} %get-tuple-element.12), channel_id=1, source_target_pairs={{0,16},{16,0},{1,17},{17,1},{2,18},{18,2},{3,19},{19,3},{4,20},{20... | collective-permute-start | bytes 786440 | tf_op jit(solution)/shard_map/ppermute | solution.py:337

commit v2 on v1

v2 whole, which is shorter than its diff:
```python
import functools
import math

import jax
import jax.numpy as jnp
import ml_dtypes
import numpy as np
from jax import lax
from jax.experimental import pallas as pl
from jax.experimental.pallas import tpu as pltpu
from jax.sharding import Mesh
from jax.sharding import PartitionSpec as P

LAGS = 512
BAND = 128
TILE_ROWS = 16
TILE_COLS = 8
TILE_SLOTS = 4
PER_TILE = TILE_ROWS + TILE_COLS
REFS = TILE_SLOTS * PER_TILE
PAIRS = TILE_ROWS * TILE_COLS
CAP = 6
GROUPS = 4
CHUNK = CAP * GROUPS
STEPS = 4
SEND_VMEM = 60 * 1024 * 1024
STACK_VMEM = 48 * 1024 * 1024
HALF = LAGS // 2
F32 = jnp.float32
BF16 = jnp.bfloat16


def iota(shape, dim):
    return lax.broadcasted_iota(jnp.int32, shape, dim)


def before(size):
    return (iota((size, size), 0) < iota((size, size), 1)).astype(BF16)


def send_kernel(
    home_in, block_in, chan_in, raw_ref, out_ref,
    rows_ref, sent_ref, home_ref, block_ref, chan_ref, sems, small_sems, out_sems,
):
    owners = block_ref.shape[0]
    _, channels, width = raw_ref.shape
    bins = width // 2
    wide = bins // STEPS
    sub = wide // GROUPS
    copies = []
    for k in range(STEPS):
        for half in range(2):
            lanes = pl.ds(half * bins + k * wide, wide)
            copy = pltpu.make_async_copy(
                raw_ref.at[0, :, lanes], rows_ref.at[:, lanes], sems.at[2 * k + half]
            )
            copies.append(copy)
    small = [
        pltpu.make_async_copy(source, target, small_sems.at[i])
        for i, (source, target) in enumerate(
            ((home_in, home_ref), (block_in, block_ref), (chan_in, chan_ref))
        )
    ]
    for copy in small + copies:
        copy.start()
    for copy in small:
        copy.wait()

    me = lax.axis_index("pairs")
    block = jnp.int32(0)
    for b in range(owners):
        block = jnp.where(block_ref[b] == me, b, block)
    chan = chan_ref[...]
    offset = iota((PER_TILE, channels), 1) + block * channels
    owner = iota((owners, channels), 0)
    named = jnp.zeros((owners, channels), F32)
    for t in range(home_ref.shape[0]):
        hit = jnp.max((chan[:, t : t + 1] == offset).astype(F32), axis=0, keepdims=True)
        named = jnp.maximum(named, jnp.where(owner == home_ref[t], hit, 0.0))
    rank = jnp.dot(named.astype(BF16), before(channels), preferred_element_type=F32)
    key = jnp.where(named > 0.0, rank, -1.0)
    row = iota((CHUNK, channels), 0)
    place = (row % CAP).astype(F32)
    group = row // CAP
    parts = []
    for p in range(owners):
        match = jnp.broadcast_to(key[p : p + 1, :], (CHUNK, channels)) == place
        parts.append(
            jnp.concatenate(
                [jnp.where(match & (group == g), 1.0, 0.0) for g in range(GROUPS)], axis=1
            )
        )
    pick = jnp.concatenate(parts, axis=0).astype(BF16)

    outs = []
    for k in range(STEPS):
        copies[2 * k].wait()
        copies[2 * k + 1].wait()
        stacked = []
        for g in range(GROUPS):
            first = k * wide + g * sub
            stacked.append(
                jnp.concatenate(
                    [rows_ref[:, first : first + sub], rows_ref[:, bins + first : bins + first + sub]],
                    axis=1,
                )
            )
        stacked = jnp.concatenate(stacked, axis=0)
        lanes = slice(2 * k * sub, 2 * (k + 1) * sub)
        sent_ref[:, lanes] = jnp.dot(pick, stacked, preferred_element_type=F32).astype(BF16)
        copy = pltpu.make_async_copy(sent_ref.at[:, lanes], out_ref.at[:, lanes], out_sems.at[k])
        copy.start()
        outs.append(copy)
    for copy in outs:
        copy.wait()


def send_rows(raw, chan, tile_home, block_home):
    _, channels, width = raw.shape
    owners = block_home.shape[0]
    anywhere = pl.BlockSpec(memory_space=pl.ANY)
    shape = (owners * CHUNK, width // GROUPS)
    return pl.pallas_call(
        send_kernel,
        in_specs=[anywhere] * 4,
        out_specs=anywhere,
        out_shape=jax.ShapeDtypeStruct(shape, BF16),
        scratch_shapes=[
            pltpu.VMEM((channels, width), BF16),
            pltpu.VMEM(shape, BF16),
            pltpu.SMEM(tile_home.shape, jnp.int32),
            pltpu.SMEM(block_home.shape, jnp.int32),
            pltpu.VMEM(chan.shape, jnp.int32),
            pltpu.SemaphoreType.DMA((2 * STEPS,)),
            pltpu.SemaphoreType.DMA((3,)),
            pltpu.SemaphoreType.DMA((STEPS,)),
        ],
        compiler_params=pltpu.CompilerParams(vmem_limit_bytes=SEND_VMEM),
        name="send_rows",
    )(tile_home, block_home, chan, raw)


def table_kernel(scale, home_ref, block_ref, chan_ref, lag_ref, place_ref, cos_ref, sin_ref):
    step = pl.program_id(0)
    rows = lag_ref.shape[0]
    low = cos_ref.shape[0]
    high = rows // low
    turn = 2 * rows * STEPS

    def angles(count, first, stride):
        freq = (iota((count, HALF), 0) + first) * stride
        lag = iota((count, HALF), 1) + 1
        return ((freq * lag) & (turn - 1)).astype(F32) * (2.0 * math.pi / turn)

    @pl.when(step == 0)
    def _():
        angle = angles(low, 0, 1)
        cos_ref[...] = jnp.cos(angle)
        sin_ref[...] = jnp.sin(angle)
        me = lax.axis_index("pairs")
        core = lax.axis_index("core")
        chan = chan_ref[...]
        lane = iota(chan.shape, 1)
        columns = []
        for s in range(TILE_SLOTS):
            tile = jnp.int32(-1)
            seen = jnp.int32(0)
            for t in range(home_ref.shape[0]):
                mine = home_ref[t] == me
                tile = jnp.where(mine & (seen == s), t, tile)
                seen = seen + mine.astype(jnp.int32)
            column = jnp.sum(jnp.where(lane == tile, chan + 1, 0), axis=1, keepdims=True) - 1
            sides = [
                jnp.concatenate(
                    [column[i : i + 2] for i in range(2 * c, TILE_ROWS, 4)], axis=0
                )
                for c in range(2)
            ]
            columns.append(jnp.where(core == 0, sides[0], sides[1]))
            columns.append(jnp.where(core == 0, sides[1], sides[0]))
            columns.append(column[TILE_ROWS:])
        named = jnp.broadcast_to(jnp.concatenate(columns, axis=0), (REFS, BAND))
        cell = iota((REFS, BAND), 1)
        in_block = (named >= 0) & ((named // BAND) == cell)
        at_offset = (named >= 0) & ((named % BAND) == cell)
        block_hot = in_block.astype(F32).astype(BF16)
        offset_hot = at_offset.astype(F32)
        count = lax.dot_general(
            block_hot, offset_hot.astype(BF16), (((0,), (0,)), ((), ())), preferred_element_type=F32
        )
        rank = jnp.dot(
            (count > 0.0).astype(F32).astype(BF16), before(BAND), preferred_element_type=F32
        )
        own_rank = jnp.dot(block_hot, rank.astype(BF16), preferred_element_type=F32)
        position = jnp.sum(own_rank * offset_hot, axis=1, keepdims=True).astype(jnp.int32)
        holder = jnp.zeros((REFS, BAND), jnp.int32)
        for b in range(block_ref.shape[0]):
            holder = jnp.where((named // BAND) == b, block_ref[b], holder)
        place_ref[...] = jnp.where(named >= 0, holder * CHUNK + position, -CHUNK)

    coarse = angles(high, step * high, low)
    cos_high = jnp.cos(coarse) * scale
    sin_high = jnp.sin(coarse) * scale
    cos_low = cos_ref[...]
    sin_low = sin_ref[...]
    for q in range(high):
        ch = cos_high[q : q + 1, :]
        sh = sin_high[q : q + 1, :]
        rows_q = slice(q * low, (q + 1) * low)
        lag_ref[rows_q, :HALF] = (ch * cos_low - sh * sin_low).astype(BF16)
        lag_ref[rows_q, HALF:] = (sh * cos_low + ch * sin_low).astype(BF16)


def tables(bins, segments, chan, tile_home, block_home):
    rows = bins // STEPS
    low = 64
    return pl.pallas_call(
        functools.partial(table_kernel, 1.0 / math.sqrt(bins * segments)),
        grid=(STEPS,),
        in_specs=[
            pl.BlockSpec(memory_space=pltpu.SMEM),
            pl.BlockSpec(memory_space=pltpu.SMEM),
            pl.BlockSpec(chan.shape, lambda i: (0, 0)),
        ],
        out_specs=[
            pl.BlockSpec((rows, LAGS), lambda i: (i, 0)),
            pl.BlockSpec((REFS, BAND), lambda i: (0, 0)),
        ],
        out_shape=[
            jax.ShapeDtypeStruct((bins, LAGS), BF16),
            jax.ShapeDtypeStruct((REFS, BAND), jnp.int32),
        ],
        scratch_shapes=[pltpu.VMEM((low, HALF), F32), pltpu.VMEM((low, HALF), F32)],
        compiler_params=pltpu.CompilerParams(vmem_limit_bytes=32 * 1024 * 1024),
        cost_estimate=pl.CostEstimate(flops=20_000_000, bytes_accessed=8_000_000, transcendentals=0),
        name="tables",
    )(tile_home, block_home, chan)


def stack_kernel(
    zero_scale, place_ref, got_ref, lag_ref, keep_ref, send_ref,
    cross_re0, cross_im0, cross_re1, cross_im1, cross_re2, cross_im2, cross_re3, cross_im3, even_ref, odd_ref, zero_ref, chosen_ref,
    table_ref, sems,
):
    received, width = got_ref.shape
    wide = lag_ref.shape[0] // STEPS
    copies = []
    for k in range(STEPS):
        span = pl.ds(k * wide, wide)
        copy = pltpu.make_async_copy(lag_ref.at[span], table_ref.at[span], sems.at[k])
        copy.start()
        copies.append(copy)
    sub = wide // GROUPS
    crosses = [
        (cross_re0, cross_im0), (cross_re1, cross_im1), (cross_re2, cross_im2), (cross_re3, cross_im3)
    ]

    place = place_ref[...]
    column = iota((REFS, BAND), 1)
    for g in range(GROUPS):
        chosen_ref[g * REFS : (g + 1) * REFS, :] = jnp.concatenate(
            [
                jnp.where(column + k * BAND == place + g * CAP, 1.0, 0.0)
                for k in range(received // BAND)
            ],
            axis=1,
        ).astype(BF16)

    def multiply(k, half):
        total, lanes = ((even_ref, slice(0, HALF)), (odd_ref, slice(HALF, LAGS)))[half]
        product = jnp.dot(
            crosses[k][half][...],
            table_ref[k * wide : (k + 1) * wide, lanes],
            preferred_element_type=F32,
        )
        total[...] = product if k == 0 else total[...] + product

    for k in range(STEPS):
        if k == 2:
            for copy in copies:
                copy.wait()
        white_re, white_im = [], []
        for band in range(sub // BAND):
            first = 2 * k * sub + band * BAND
            re = got_ref[:, first : first + BAND].astype(F32)
            im = got_ref[:, first + sub : first + sub + BAND].astype(F32)
            power = jnp.sum(re * re + im * im, axis=1, keepdims=True) * (1.0 / BAND)
            scale = lax.rsqrt(power + 1e-06)
            white_re.append((re * scale).astype(BF16))
            white_im.append((im * scale).astype(BF16))
        white = jnp.concatenate(white_re + white_im, axis=1)
        rows = jnp.dot(chosen_ref[...], white, preferred_element_type=F32)
        cross_re, cross_im = crosses[k]
        for g in range(GROUPS):
            for s in range(TILE_SLOTS):
                top = g * REFS + s * PER_TILE
                b_re = rows[top + TILE_ROWS : top + PER_TILE, :sub]
                b_im = rows[top + TILE_ROWS : top + PER_TILE, sub:]
                for side in range(2):
                    re_parts, im_parts = [], []
                    for i in range(side * TILE_ROWS // 2, (side + 1) * TILE_ROWS // 2):
                        a_re = rows[top + i : top + i + 1, :sub]
                        a_im = rows[top + i : top + i + 1, sub:]
                        re_parts.append(a_re * b_re + a_im * b_im)
                        im_parts.append(a_re * b_im - a_im * b_re)
                    re_all = jnp.concatenate(re_parts, axis=0)
                    im_all = jnp.concatenate(im_parts, axis=0)
                    first = (side * TILE_SLOTS + s) * PAIRS // 2
                    span = slice(first, first + PAIRS // 2)
                    folded = re_all[:, :BAND]
                    for band in range(1, sub // BAND):
                        folded = folded + re_all[:, band * BAND : (band + 1) * BAND]
                    zero_ref[span, :] = folded if k + g == 0 else zero_ref[span, :] + folded
                    cross_re[span, g * sub : (g + 1) * sub] = re_all.astype(BF16)
                    cross_im[span, g * sub : (g + 1) * sub] = im_all.astype(BF16)
            if k == 2:
                multiply(g // 2, g % 2)
            if k == 3 and g % 2 == 1:
                multiply(2, g // 2)
    multiply(STEPS - 1, 0)
    multiply(STEPS - 1, 1)

    mirror = (iota((HALF, HALF), 0) + iota((HALF, HALF), 1) == HALF - 1).astype(F32).astype(BF16)
    rows_each = even_ref.shape[0] // 2
    for side, out_ref in enumerate((keep_ref, send_ref)):
        span = slice(side * rows_each, (side + 1) * rows_each)
        even = even_ref[span, :]
        odd = odd_ref[span, :]
        behind = even + odd
        high = behind.astype(BF16)
        mirrored = jnp.dot(high, mirror, preferred_element_type=F32)
        if side == 0:
            low = (behind - high.astype(F32)).astype(BF16)
            mirrored = mirrored + jnp.dot(low, mirror, preferred_element_type=F32)
        ahead = pltpu.roll(even - odd, 1, 1)
        at_zero = jnp.sum(zero_ref[span, :], axis=1, keepdims=True) * zero_scale
        ahead = jnp.where(iota(ahead.shape, 1) == 0, at_zero, ahead)
        out_ref[:, :HALF] = mirrored.astype(out_ref.dtype)
        out_ref[:, HALF:] = ahead.astype(out_ref.dtype)


def stack(place, got, lag, segments):
    received, _ = got.shape
    bins = lag.shape[0]
    pairs = TILE_SLOTS * PAIRS
    zero_scale = float(np.float32(1.0 / math.sqrt(bins * segments)).astype(ml_dtypes.bfloat16))
    shape = (pairs // 2, LAGS)
    vmem = pl.BlockSpec(memory_space=pltpu.VMEM)
    return pl.pallas_call(
        functools.partial(stack_kernel, zero_scale),
        in_specs=[vmem, vmem, pl.BlockSpec(memory_space=pl.ANY)],
        out_specs=[vmem] * 2,
        out_shape=[jax.ShapeDtypeStruct(shape, F32), jax.ShapeDtypeStruct(shape, BF16)],
        scratch_shapes=[pltpu.VMEM((pairs, bins // STEPS), BF16)] * (2 * STEPS)
        + [
            pltpu.VMEM((pairs, HALF), F32),
            pltpu.VMEM((pairs, HALF), F32),
            pltpu.VMEM((pairs, BAND), F32),
            pltpu.VMEM((GROUPS * REFS, received), BF16),
            pltpu.VMEM(lag.shape, BF16),
            pltpu.SemaphoreType.DMA((STEPS,)),
        ],
        compiler_params=pltpu.CompilerParams(vmem_limit_bytes=STACK_VMEM),
        name="stack",
    )(place, got, lag)


def shards(raw_spectra, tile_chan, tile_home, block_home):
    depth = lax.axis_size("z")
    segments = 2 * depth
    bins = raw_spectra.shape[2] // 2
    chan = tile_chan.T
    outgoing = send_rows(raw_spectra, chan, tile_home, block_home)
    owners = block_home.shape[0]
    incoming = lax.all_to_all(
        outgoing.reshape(owners, CHUNK, -1), "pairs", split_axis=0, concat_axis=0, tiled=True
    )
    lag, place = tables(bins, segments, chan, tile_home, block_home)
    keep, send = stack(place, incoming.reshape(outgoing.shape), lag, segments)
    swapped = lax.ppermute(send, "core", [(0, 1), (1, 0)])
    both = (keep + swapped.astype(F32)).astype(BF16).reshape(depth, -1, LAGS)
    parts = lax.all_to_all(both, "z", split_axis=0, concat_axis=0, tiled=True)
    return jnp.sum(parts.astype(F32), axis=0)[None]


def solution(mesh):
    devices = mesh.devices
    split = Mesh(
        devices.reshape(devices.shape[0] // 2, 2, devices.shape[1]), ("z", "core", "pairs")
    )
    return jax.shard_map(
        shards,
        mesh=split,
        in_specs=(P(("z", "core"), "pairs", None), P(), P(), P()),
        out_specs=P("pairs", ("z", "core"), None),
        check_vma=False,
    )
```

time: 84.9 us -> 79.4 us (0.935)
  local copies, waits for them, and re-layouts: 5.56 us -> 1.96 us
  Pallas kernels: 15.2 us -> 12.9 us
    unnamed x16 -> x8, local copies, waits for them, and re-layouts: 5.56 us -> 1.96 us
    pallas_call x3 -> x2, Pallas kernels: 12.2 us -> 9.85 us  [the longest x1 5.75 us: stack(): pl.pallas_call(functools.partial(stack_kernel, zero_scale), in_specs=[vme...]
where the time goes in v2:
time: 79.4 us; the launch traced here: 79.1 us
  blocking collectives  33.4 us (42%)
  waiting for transfers between devices  20.9 us (26%)
  Pallas kernels  12.9 us (16%)
  starting transfers between devices  9.1 us (11%)
  local copies, waits for them, and re-layouts  1.96 us (2%)
    all_to_all x1, blocking collectives, shards(): parts = lax.all_to_all(both, 'z', split_axis=0, concat_axis=0, tiled=True)  33.4 us
    all_to_all x1, waiting for transfers between devices, shards(): lax.all_to_all(outgoing.reshape(owners, CHUNK, -1), 'pairs', split_axis=0...  19.4 us
    all_to_all x1, starting transfers between devices, shards(): lax.all_to_all(outgoing.reshape(owners, CHUNK, -1), 'pairs', split_axis=0...  7.17 us
    pallas_call x1, Pallas kernels, stack(): pl.pallas_call(functools.partial(stack_kernel, zero_scale), in_specs=[vme...  5.75 us
    pallas_call x1, Pallas kernels, send_rows(): pl.pallas_call(send_kernel, in_specs=[anywhere] * 4, out_specs=anywhere,...  4.1 us
    pallas_call x1, Pallas kernels, tables(): pl.pallas_call(functools.partial(table_kernel, 1.0 / math.sqrt(bins * seg...  3.09 us
    unnamed x8, local copies, waits for them, and re-layouts  1.96 us
    ppermute x1, starting transfers between devices, shards(): swapped = lax.ppermute(send, 'core', [(0, 1), (1, 0)])  1.92 us
  transfers between devices with their start and end apart: 2, of which 2 were waited for; matrix products, arithmetic and copies ran while one was open for 0% of the time, Pallas kernels for 4%

profile of v2, /device:TPU:32, one launch (start us, length us, event | category | flops | bytes accessed | tf_op | source)
XLA Modules:
  0.0 79.1 jit_solution(13110071320037170505)
XLA Ops:
  0.0 4.1 %send_rows.1 = bf16[384,2048]{1,0:T(8,128)(2,1)} custom-call(s32[28]{0:T(128)} %home_in.1, s32[16]{0:T(128)} %block_in.1, s32[24,28]{1,0:T(8,128)} %bitcast.6, bf16[1,128,8192]{2,1,0:T(8,128)(2,1)} %raw_ref.1), custom_call_target="tpu_custom_call" | custom-call | tf_op jit(solution)/shard_map/send_rows/pallas_call | solution.py:123
  4.1 0.0 copy-start.1
  4.1 0.0 copy-start.2
  4.1 0.0 copy-start.3
  4.1 7.2 %all-to-all-start = ((bf16[16,24,2048]{2,1,0:T(8,128)(2,1)}), bf16[16,24,2048]{2,1,0:T(8,128)(2,1)S(1)}, u32[]{:S(2)}, u32[]{:S(2)}) async-start(bf16[16,24,2048]{2,1,0:T(8,128)(2,1)} %bitcast.8), calls=%async_computation | async-start | bytes 3145728 | tf_op jit(solution)/shard_map/all_to_all | solution.py:375
  11.3 0.0 copy-done.1
  11.3 0.0 copy-done.2
  11.3 0.0 copy-done.3
  11.4 3.1 %tables.1 = (bf16[4096,512]{1,0:T(8,128)(2,1)S(1)}, s32[96,128]{1,0:T(8,128)S(1)}) custom-call(s32[28]{0:T(128)S(1)} %copy-done.2, s32[16]{0:T(128)S(1)} %copy-done.3, s32[24,28]{1,0:T(8,128)S(1)} %bitcast.7), custom_call_target="tpu_custom_call" | custom-call | flops 20000000 | bytes 8000000 | tf_op jit(solution)/shard_map/tables/pallas_call | solution.py:217
  14.5 0.0 copy-start
  14.5 1.9 %copy-done = bf16[4096,512]{1,0:T(8,128)(2,1)} copy-done((bf16[4096,512]{1,0:T(8,128)(2,1)}, bf16[4096,512]{1,0:T(8,128)(2,1)S(1)}, u32[]{:S(2)}) %copy-start) | copy-done | bytes 4194328
  16.4 19.4 %all-to-all-done = bf16[16,24,2048]{2,1,0:T(8,128)(2,1)S(1)} async-done(((bf16[16,24,2048]{2,1,0:T(8,128)(2,1)}), bf16[16,24,2048]{2,1,0:T(8,128)(2,1)S(1)}, u32[]{:S(2)}, u32[]{:S(2)}) %all-to-all-start) | async-done | bytes 1572896 | tf_op jit(solution)/shard_map/all_to_all | solution.py:375
  35.8 5.8 %stack.1 = (f32[256,512]{1,0:T(8,128)S(1)}, bf16[256,512]{1,0:T(8,128)(2,1)S(1)}) custom-call(s32[96,128]{1,0:T(8,128)S(1)} %get-tuple-element.9.place_ref, bf16[384,2048]{1,0:T(8,128)(2,1)S(1)} %bitcast.5, bf16[4096,512]{1,0:T(8,128)(2,1)} %copy-done), custom_call_target="tpu_custom_call" | custom-call | tf_op jit(solution)/shard_map/stack/pallas_call | solution.py:349
  41.5 1.9 %collective-permute-start = (bf16[256,512]{1,0:T(8,128)(2,1)S(1)}, bf16[256,512]{1,0:T(8,128)(2,1)S(1)}, u32[]{:S(2)}, u32[]{:S(2)}) collective-permute-start(bf16[256,512]{1,0:T(8,128)(2,1)S(1)} %get-tuple-element.12), channel_id=1, source_target_pairs={{0,16},{16,0},{1,17},{17,1},{2,18},{18,2},{3,19},{19,3},{4,20},{20... | collective-permute-start | bytes 786440 | tf_op jit(solution)/shard_map/ppermute | solution.py:380
  43.5 1.5 %collective-permute-done = bf16[256,512]{1,0:T(8,128)(2,1)S(1)} collective-permute-done((bf16[256,512]{1,0:T(8,128)(2,1)S(1)}, bf16[256,512]{1,0:T(8,128)(2,1)S(1)}, u32[]{:S(2)}, u32[]{:S(2)}) %collective-permute-start) | collective-permute-done | bytes 262176 | tf_op jit(solution)/shard_map/ppermute | solution.py:380
  45.0 0.1 add_convert_fusion
  45.1 33.4 %all_to_all.10 = bf16[16,16,512]{2,1,0:T(8,128)(2,1)S(1)} all-to-all(bf16[16,16,512]{2,1,0:T(8,128)(2,1)S(1)} %bitcast.9), channel_id=1, replica_groups=mesh['z'=16,'core'=2,'pairs'=16] {'z'}, dimensions={0} | all-to-all | bytes 524288 | tf_op jit(solution)/shard_map/all_to_all | solution.py:382
  78.4 0.7 convert_reduce_fusion
Async XLA Ops:
  4.1 7.2 %copy-start.1 = (s32[28,24]{0,1:T(8,128)S(1)}, s32[28,24]{0,1:T(8,128)}, u32[]{:S(2)}) copy-start(s32[28,24]{0,1:T(8,128)} %param.5) | copy-start | bytes 8068
  4.1 7.2 %copy-start.2 = (s32[28]{0:T(128)S(1)}, s32[28]{0:T(128)}, u32[]{:S(2)}) copy-start(s32[28]{0:T(128)} %home_in.1) | copy-start | bytes 340
  4.1 7.2 %copy-start.3 = (s32[16]{0:T(128)S(1)}, s32[16]{0:T(128)}, u32[]{:S(2)}) copy-start(s32[16]{0:T(128)} %block_in.1) | copy-start | bytes 196
  4.1 31.6 %all-to-all-start = ((bf16[16,24,2048]{2,1,0:T(8,128)(2,1)}), bf16[16,24,2048]{2,1,0:T(8,128)(2,1)S(1)}, u32[]{:S(2)}, u32[]{:S(2)}) async-start(bf16[16,24,2048]{2,1,0:T(8,128)(2,1)} %bitcast.8), calls=%async_computation | async-start | bytes 3145728 | tf_op jit(solution)/shard_map/all_to_all | solution.py:375
  14.5 1.9 %copy-start = (bf16[4096,512]{1,0:T(8,128)(2,1)}, bf16[4096,512]{1,0:T(8,128)(2,1)S(1)}, u32[]{:S(2)}) copy-start(bf16[4096,512]{1,0:T(8,128)(2,1)S(1)} %get-tuple-element.10.lag_ref) | copy-start | bytes 12582916
  41.5 3.4 %collective-permute-start = (bf16[256,512]{1,0:T(8,128)(2,1)S(1)}, bf16[256,512]{1,0:T(8,128)(2,1)S(1)}, u32[]{:S(2)}, u32[]{:S(2)}) collective-permute-start(bf16[256,512]{1,0:T(8,128)(2,1)S(1)} %get-tuple-element.12), channel_id=1, source_target_pairs={{0,16},{16,0},{1,17},{17,1},{2,18},{18,2},{3,19},{19,3},{4,20},{20... | collective-permute-start | bytes 786440 | tf_op jit(solution)/shard_map/ppermute | solution.py:380
